TPU v7x, 32 devices: a whole 2x2x4 slice. The times are simulated.
32 devices in a mesh: lat: 4 (over y, core), lon: 8 (over z, x).
Axes of the slice: x: 2, y: 2, z: 4, core: 2. Of those that a mesh axis runs over, the one named last changes fastest.
Arguments:
- tracers: bfloat16 [4, 12, 256, 1024], P(None, None, 'lat', 'lon'), may hold values from -6 to 6
- weights: bfloat16 [256, 2, 1024, 128], P('lat', None, 'lon'), may hold values from -0.375 to 0.375
- src_row: int32 [256, 8, 2], P('lat', 'lon'), may hold values from 0 to 255, as said below
- src_sector: int32 [256, 8, 2], P('lat', 'lon'), may hold values from 0 to 7, as said below
- kv: float32 [11, 256, 1024], P(None, 'lat', 'lon'), may hold values from 0.02 to 0.24
- kh: float32 [256, 1024], P('lat', 'lon'), may hold values from 0.03 to 0.24
Outputs:
- advected_tracers: bfloat16 [4, 12, 256, 1024], P(None, None, 'lat', 'lon')
Inputs may be any that keep to these rules, and one draw needn't show every extreme that they name: src_row[y, j, k] lies within 3 rows of y and in the latitude band of row y, from 64 * (y // 64) to 64 * (y // 64) + 63. src_sector[y, j, k] is within 2 sectors of j, periodically; among the 128 entries of one band and sector j, at most 32 name the same sector, and in every band and sector some sector is named exactly 32 times.
All inputs are finite; a program needn't handle non-finite values.
Results may differ from a plain program's by a relative error of at most 0.0049.
Values may be sent and summed in bfloat16 or wider, within the bound.
A program may use at most 64 MiB of HBM per device.

v0:
```python
import jax
import jax.numpy as jnp
from jax import lax
from jax.sharding import PartitionSpec as P

STEPS = 2
SUBSTEPS = 2


def passed_along(x, axis, by):
    size = lax.axis_size(axis)
    return lax.ppermute(x, axis, [(i, (i + by) % size) for i in range(size)])


def padded(block, sides, width, periodic):
    for axis, dim in sides:
        count = lax.axis_size(axis)
        forward = [(i, i + 1) for i in range(count - 1)]
        if periodic:
            forward.append((count - 1, 0))
        backward = [(target, source) for source, target in forward]
        low = lax.ppermute(
            lax.slice_in_dim(block, block.shape[dim] - width, None, axis=dim), axis, forward
        )
        high = lax.ppermute(lax.slice_in_dim(block, 0, width, axis=dim), axis, backward)
        block = jnp.concatenate([low, block, high], axis=dim)
    return block


def vertical(advected, kv):
    flux = kv[None] * (advected[:, 1:] - advected[:, :-1])
    zero_flux = jnp.zeros_like(flux[:, :1])
    return (
        advected
        + jnp.concatenate([flux, zero_flux], axis=1)
        - jnp.concatenate([zero_flux, flux], axis=1)
    )


def relax(extended, coef):
    center = extended[:, :, 1:-1, 1:-1]
    beside_all = (
        extended[:, :, :-2, 1:-1]
        + extended[:, :, 2:, 1:-1]
        + extended[:, :, 1:-1, :-2]
        + extended[:, :, 1:-1, 2:]
    )
    return center + coef * (beside_all - 4.0 * center)


def local(tracers, weights, src_row, src_sector, kv, kh):
    tracer_count, level_count, tile_rows, tile_cols = tracers.shape
    channels = tracer_count * level_count
    sectors = lax.axis_size("lon")
    band_index = lax.axis_index("lat")
    sector_index = lax.axis_index("lon")
    reach = src_row.shape[2]
    request_count = tile_rows * reach
    wanted_rows = src_row.reshape(request_count) - band_index * tile_rows
    wanted_sectors = src_sector.reshape(request_count)
    nearby = (wanted_sectors - sector_index + 2 + sectors) % sectors
    picks = nearby * tile_rows + wanted_rows
    field = tracers
    for step in range(STEPS):
        flat = field.reshape(channels, tile_rows, tile_cols)
        pieces = []
        for offset in (-2, -1, 0, 1, 2):
            if offset == 0:
                pieces.append(flat)
            else:
                pieces.append(passed_along(flat, "lon", -offset))
        stacked = jnp.concatenate(pieces, axis=1)
        source = jnp.take(stacked, picks, axis=1)
        source = source.reshape(channels, tile_rows, reach, tile_cols)
        advected = jnp.einsum("cykq,ykpq->cyp", source, weights, preferred_element_type=jnp.float32)
        advected = advected.reshape(tracer_count, level_count, tile_rows, tile_cols)
        smoothed = vertical(advected, kv)
        for substep in range(SUBSTEPS):
            extended = padded(smoothed, (("lon", 3),), 1, True)
            extended = padded(extended, (("lat", 2),), 1, False)
            smoothed = relax(extended, kh)
        field = smoothed.astype(jnp.bfloat16)
    return field


def solution(mesh):
    return jax.shard_map(
        local,
        mesh=mesh,
        in_specs=(
            P(None, None, "lat", "lon"),
            P("lat", None, "lon", None),
            P("lat", "lon", None),
            P("lat", "lon", None),
            P(None, "lat", "lon"),
            P("lat", "lon"),
        ),
        out_specs=P(None, None, "lat", "lon"),
        check_vma=False,
    )
```

profile of v0, /device:TPU:0, one launch (start us, length us, event | category | flops | bytes accessed | tf_op | source)
XLA Modules:
  0.0 235.4 jit_solution(7025346697768602759)
XLA Ops:
  0.0 1.7 copy.39
  1.7 3.1 %collective-permute-start = (bf16[48,64,128]{2,0,1:T(8,128)(2,1)S(1)}, bf16[48,64,128]{2,0,1:T(8,128)(2,1)}, u32[]{:S(2)}, u32[]{:S(2)}) collective-permute-start(bf16[48,64,128]{2,0,1:T(8,128)(2,1)S(1)} %copy.39), channel_id=1, source_target_pairs={{0,2},{1,3},{2,4},{3,5},{4,6},{5,7},{6,0},{7,1},{8,10},{9,11},{10,... | collective-permute-start | bytes 2359304 | tf_op jit(solution)/shard_map/ppermute | solution.py:12
  6.2 3.2 %collective-permute-start.2 = (bf16[48,64,128]{2,0,1:T(8,128)(2,1)S(1)}, bf16[48,64,128]{2,0,1:T(8,128)(2,1)S(1)}, u32[]{:S(2)}, u32[]{:S(2)}) collective-permute-start(bf16[48,64,128]{2,0,1:T(8,128)(2,1)S(1)} %copy.39), channel_id=1, source_target_pairs={{0,7},{1,0},{2,1},{3,2},{4,3},{5,4},{6,5},{7,6},{8,15},{9,8},{10,9... | collective-permute-start | bytes 2359304 | tf_op jit(solution)/shard_map/ppermute | solution.py:12
  10.3 15.0 %collective-permute-done = bf16[48,64,128]{2,0,1:T(8,128)(2,1)} collective-permute-done((bf16[48,64,128]{2,0,1:T(8,128)(2,1)S(1)}, bf16[48,64,128]{2,0,1:T(8,128)(2,1)}, u32[]{:S(2)}, u32[]{:S(2)}) %collective-permute-start) | collective-permute-done | bytes 786464 | tf_op jit(solution)/shard_map/ppermute | solution.py:12
  25.3 2.1 constant_dynamic-update-slice_fusion.4
  27.4 15.8 %collective-permute-done.1 = bf16[48,64,128]{2,0,1:T(8,128)(2,1)S(1)} collective-permute-done((bf16[48,64,128]{2,0,1:T(8,128)(2,1)S(1)}, bf16[48,64,128]{2,0,1:T(8,128)(2,1)S(1)}, u32[]{:S(2)}, u32[]{:S(2)}) %collective-permute-start.1) | collective-permute-done | bytes 786464 | tf_op jit(solution)/shard_map/ppermute | solution.py:12
  46.5 11.5 %collective-permute-done.3 = bf16[48,64,128]{2,0,1:T(8,128)(2,1)S(1)} collective-permute-done((bf16[48,64,128]{2,0,1:T(8,128)(2,1)S(1)}, bf16[48,64,128]{2,0,1:T(8,128)(2,1)S(1)}, u32[]{:S(2)}, u32[]{:S(2)}) %collective-permute-start.3) | collective-permute-done | bytes 786464 | tf_op jit(solution)/shard_map/ppermute | solution.py:12
  59.0 3.0 %gather_fusion = bf16[128,48,128]{2,1,0:T(8,128)(2,1)S(1)} fusion(bf16[48,320,128]{2,0,1:T(8,128)(2,1)} %constant_dynamic-update-slice_fusion, s32[1024]{0:T(1024)S(1)} %pad_clamp_fusion), kind=kCustom, calls=%fused_computation.clone | custom fusion | bytes 3146240 | tf_op jit(solution)/shard_map/jit(_take)/gather | solution.py:73
  62.2 3.7 %convolution_bitcast_fusion.1 = f32[48,64,128]{2,0,1:T(8,128)S(1)} fusion(bf16[48,64,2,128]{3,0,2,1:T(8,128)(2,1)S(1)} %bitcast.35, bf16[64,2,128,128]{3,2,1,0:T(8,128)(2,1)} %param.9), kind=kOutput, calls=%fused_computation.65 | convolution fusion | flops 201326592 | bytes 7340032 | tf_op jit(solution)/shard_map/cykq,ykpq->cyp/dot_general | solution.py:75
  67.4 1.8 fusion.34
  69.2 1.9 copy.45
  71.1 1.5 collective-permute-start.4
  73.8 3.2 %collective-permute-start.5 = (f32[4,12,64,1]{2,0,3,1:T(4,128)}, f32[4,12,64,1]{2,0,3,1:T(4,128)}, u32[]{:S(2)}, u32[]{:S(2)}) collective-permute-start(f32[4,12,64,1]{2,0,3,1:T(4,128)} %copy.46), channel_id=1, source_target_pairs={{1,0},{2,1},{3,2},{4,3},{5,4},{6,5},{7,6},{0,7},{9,8},{10,9},{11,1... | collective-permute-start | bytes 36872 | tf_op jit(solution)/shard_map/ppermute | solution.py:25
  78.8 2.5 %copy.48 = f32[4,12,64,1]{3,2,1,0:T(8,128)} copy(f32[4,12,64,1]{2,0,3,1:T(4,128)} %collective-permute-done.5) | data formatting | bytes 24576 | tf_op jit(solution)/shard_map/ppermute | solution.py:25
  81.2 1.5 pad_maximum_fusion.43
  85.4 3.6 %collective-permute-done.7 = f32[4,12,1,130]{3,2,1,0:T(1,128)S(1)} collective-permute-done((f32[4,12,1,130]{3,2,1,0:T(1,128)S(1)}, f32[4,12,1,130]{3,2,1,0:T(1,128)S(1)}, u32[]{:S(2)}, u32[]{:S(2)}) %collective-permute-start.7) | collective-permute-done | bytes 24992 | tf_op jit(solution)/shard_map/ppermute | solution.py:25
  89.0 5.1 %fusion.23 = f32[4,12,64,128]{3,2,1,0:T(8,128)S(1)} fusion(f32[4,12,64,128]{3,2,1,0:T(8,128)S(1)} %pad_subtract_fusion.1, f32[4,12,64,1]{3,2,1,0:T(8,128)S(1)} %copy-done.2, f32[4,12,64,1]{3,2,1,0:T(8,128)} %copy-done, f32[4,12,1,130]{3,2,1,0:T(1,128)S(1)} %collective-permute-done.7, f32[4,12,1,130]{3,2,1,0:T(1,128)S(1)} %collective-permute-done.6, ...), kind=kLoop, calls=%fused_computation.50 | loop fusion | flops 5898240 | bytes 3252992 | tf_op jit(solution)/shard_map/add | solution.py:48
  94.0 1.8 fusion.33
  95.8 2.5 %copy.51 = f32[4,12,64,1]{2,0,3,1:T(4,128)} copy(f32[4,12,64,1]{3,2,1,0:T(8,128)} %get-tuple-element.20) | data formatting | bytes 24576 | tf_op jit(solution)/shard_map/slice | solution.py:23
  100.1 4.4 %collective-permute-start.9 = (f32[4,12,64,1]{2,0,3,1:T(4,128)}, f32[4,12,64,1]{2,0,3,1:T(4,128)}, u32[]{:S(2)}, u32[]{:S(2)}) collective-permute-start(f32[4,12,64,1]{2,0,3,1:T(4,128)} %copy.52), channel_id=1, source_target_pairs={{1,0},{2,1},{3,2},{4,3},{5,4},{6,5},{7,6},{0,7},{9,8},{10,9},{11,1... | collective-permute-start | bytes 36872 | tf_op jit(solution)/shard_map/ppermute | solution.py:25
  106.9 2.5 %copy.54 = f32[4,12,64,1]{3,2,1,0:T(8,128)} copy(f32[4,12,64,1]{2,0,3,1:T(4,128)} %collective-permute-done.9) | data formatting | bytes 24576 | tf_op jit(solution)/shard_map/ppermute | solution.py:25
  109.4 1.5 pad_maximum_fusion.40
  110.9 3.7 %collective-permute-start.10 = (f32[4,12,1,130]{3,2,1,0:T(1,128)S(1)}, f32[4,12,1,130]{3,2,1,0:T(1,128)S(1)}, u32[]{:S(2)}, u32[]{:S(2)}) collective-permute-start(f32[4,12,1,130]{3,2,1,0:T(1,128)S(1)} %get-tuple-element.12), channel_id=1, source_target_pairs={{0,8},{8,16},{16,24},{1,9},{9,17},{17,25},{2,10},{10,18},{18,26},{... | collective-permute-start | bytes 74888 | tf_op jit(solution)/shard_map/ppermute | solution.py:22
  116.1 2.1 collective-permute-done.11
  118.2 2.6 %fusion.17 = bf16[4,12,64,128]{3,2,1,0:T(8,128)(2,1)S(1)} fusion(f32[4,12,64,128]{3,2,1,0:T(8,128)S(1)} %fusion.23, f32[4,12,64,1]{3,2,1,0:T(8,128)S(1)} %copy-done.3, f32[4,12,64,1]{3,2,1,0:T(8,128)S(1)} %copy.53, f32[4,12,1,130]{3,2,1,0:T(1,128)S(1)} %collective-permute-done.11, f32[4,12,1,130]{3,2,1,0:T(1,128)S(1)} %collective-permute-done.10, ...), kind=kLoop, calls=%fused_computation.36 | loop fusion | flops 6291456 | bytes 2466560 | tf_op jit(solution)/shard_map/convert_element_type | solution.py:82
  121.3 3.5 %collective-permute-start.12 = (bf16[48,64,128]{2,0,1:T(8,128)(2,1)S(1)}, bf16[48,64,128]{2,0,1:T(8,128)(2,1)S(1)}, u32[]{:S(2)}, u32[]{:S(2)}) collective-permute-start(bf16[48,64,128]{2,0,1:T(8,128)(2,1)S(1)} %copy.57), channel_id=1, source_target_pairs={{0,2},{1,3},{2,4},{3,5},{4,6},{5,7},{6,0},{7,1},{8,10},{9,11},{10,... | collective-permute-start | bytes 2359304 | tf_op jit(solution)/shard_map/ppermute | solution.py:12
  125.9 3.7 %collective-permute-start.14 = (bf16[48,64,128]{2,0,1:T(8,128)(2,1)S(1)}, bf16[48,64,128]{2,0,1:T(8,128)(2,1)S(1)}, u32[]{:S(2)}, u32[]{:S(2)}) collective-permute-start(bf16[48,64,128]{2,0,1:T(8,128)(2,1)S(1)} %copy.57), channel_id=1, source_target_pairs={{0,7},{1,0},{2,1},{3,2},{4,3},{5,4},{6,5},{7,6},{8,15},{9,8},{10,9... | collective-permute-start | bytes 2359304 | tf_op jit(solution)/shard_map/ppermute | solution.py:12
  129.6 12.3 %collective-permute-done.12 = bf16[48,64,128]{2,0,1:T(8,128)(2,1)S(1)} collective-permute-done((bf16[48,64,128]{2,0,1:T(8,128)(2,1)S(1)}, bf16[48,64,128]{2,0,1:T(8,128)(2,1)S(1)}, u32[]{:S(2)}, u32[]{:S(2)}) %collective-permute-start.12) | collective-permute-done | bytes 786464 | tf_op jit(solution)/shard_map/ppermute | solution.py:12
  142.8 18.4 %collective-permute-done.13 = bf16[48,64,128]{2,0,1:T(8,128)(2,1)S(1)} collective-permute-done((bf16[48,64,128]{2,0,1:T(8,128)(2,1)S(1)}, bf16[48,64,128]{2,0,1:T(8,128)(2,1)S(1)}, u32[]{:S(2)}, u32[]{:S(2)}) %collective-permute-start.13) | collective-permute-done | bytes 786464 | tf_op jit(solution)/shard_map/ppermute | solution.py:12
  164.5 12.8 %collective-permute-done.15 = bf16[48,64,128]{2,0,1:T(8,128)(2,1)S(1)} collective-permute-done((bf16[48,64,128]{2,0,1:T(8,128)(2,1)S(1)}, bf16[48,64,128]{2,0,1:T(8,128)(2,1)S(1)}, u32[]{:S(2)}, u32[]{:S(2)}) %collective-permute-start.15) | collective-permute-done | bytes 786464 | tf_op jit(solution)/shard_map/ppermute | solution.py:12
  178.2 3.1 %gather_fusion.1 = bf16[128,48,128]{2,1,0:T(8,128)(2,1)S(1)} fusion(bf16[48,320,128]{2,0,1:T(8,128)(2,1)} %constant_dynamic-update-slice_fusion.5, s32[1024]{0:T(1024)} %copy-done.9), kind=kCustom, calls=%fused_computation.1.clone | custom fusion | bytes 3146240 | tf_op jit(solution)/shard_map/jit(_take)/gather | solution.py:73
  181.6 3.7 %convolution_bitcast_fusion = f32[48,64,128]{2,0,1:T(8,128)S(1)} fusion(bf16[48,64,2,128]{3,0,2,1:T(8,128)(2,1)S(1)} %bitcast.34, bf16[64,2,128,128]{3,2,1,0:T(8,128)(2,1)} %param.9), kind=kOutput, calls=%fused_computation.64 | convolution fusion | flops 201326592 | bytes 7340032 | tf_op jit(solution)/shard_map/cykq,ykpq->cyp/dot_general | solution.py:75
  186.4 1.8 fusion.32
  188.1 1.9 copy.63
  190.1 2.9 %collective-permute-start.16 = (f32[4,12,64,1]{2,0,3,1:T(4,128)S(1)}, f32[4,12,64,1]{2,0,3,1:T(4,128)S(1)}, u32[]{:S(2)}, u32[]{:S(2)}) collective-permute-start(f32[4,12,64,1]{2,0,3,1:T(4,128)S(1)} %copy.63), channel_id=1, source_target_pairs={{0,1},{1,2},{2,3},{3,4},{4,5},{5,6},{6,7},{7,0},{8,9},{9,10},{10,1... | collective-permute-start | bytes 36872 | tf_op jit(solution)/shard_map/ppermute | solution.py:22
  193.5 1.9 collective-permute-start.17
  197.3 1.7 copy.66
  199.0 1.5 pad_maximum_fusion.37
  203.2 1.8 collective-permute-done.19
  205.0 5.0 %fusion.10 = f32[4,12,64,128]{3,2,1,0:T(8,128)S(1)} fusion(f32[4,12,64,128]{3,2,1,0:T(8,128)S(1)} %pad_subtract_fusion, f32[4,12,64,1]{3,2,1,0:T(8,128)S(1)} %copy-done.4, f32[4,12,64,1]{3,2,1,0:T(8,128)} %copy-done.1, f32[4,12,1,130]{3,2,1,0:T(1,128)S(1)} %collective-permute-done.19, f32[4,12,1,130]{3,2,1,0:T(1,128)S(1)} %collective-permute-done.18, ...), kind=kLoop, calls=%fused_computation.21 | loop fusion | flops 5898240 | bytes 3252992 | tf_op jit(solution)/shard_map/add | solution.py:48
  210.0 1.8 fusion.31
  211.8 1.9 copy.69
  215.2 3.8 %collective-permute-start.21 = (f32[4,12,64,1]{2,0,3,1:T(4,128)S(1)}, f32[4,12,64,1]{2,0,3,1:T(4,128)S(1)}, u32[]{:S(2)}, u32[]{:S(2)}) collective-permute-start(f32[4,12,64,1]{2,0,3,1:T(4,128)S(1)} %copy.70), channel_id=1, source_target_pairs={{1,0},{2,1},{3,2},{4,3},{5,4},{6,5},{7,6},{0,7},{9,8},{10,9},{11,1... | collective-permute-start | bytes 36872 | tf_op jit(solution)/shard_map/ppermute | solution.py:25
  221.5 1.7 copy.72
  223.3 1.5 pad_maximum_fusion.34
  224.8 3.5 %collective-permute-start.22 = (f32[4,12,1,130]{3,2,1,0:T(1,128)S(1)}, f32[4,12,1,130]{3,2,1,0:T(1,128)S(1)}, u32[]{:S(2)}, u32[]{:S(2)}) collective-permute-start(f32[4,12,1,130]{3,2,1,0:T(1,128)S(1)} %get-tuple-element.8), channel_id=1, source_target_pairs={{0,8},{8,16},{16,24},{1,9},{9,17},{17,25},{2,10},{10,18},{18,26},{... | collective-permute-start | bytes 74888 | tf_op jit(solution)/shard_map/ppermute | solution.py:22
  229.7 2.5 %collective-permute-done.23 = f32[4,12,1,130]{3,2,1,0:T(1,128)S(1)} collective-permute-done((f32[4,12,1,130]{3,2,1,0:T(1,128)S(1)}, f32[4,12,1,130]{3,2,1,0:T(1,128)S(1)}, u32[]{:S(2)}, u32[]{:S(2)}) %collective-permute-start.23) | collective-permute-done | bytes 24992 | tf_op jit(solution)/shard_map/ppermute | solution.py:25
  232.1 3.3 %fusion.4 = bf16[4,12,64,128]{3,2,1,0:T(8,128)(2,1)} fusion(f32[4,12,64,128]{3,2,1,0:T(8,128)S(1)} %fusion.10, f32[4,12,64,1]{3,2,1,0:T(8,128)S(1)} %copy-done.5, f32[4,12,64,1]{3,2,1,0:T(8,128)S(1)} %copy.71, f32[4,12,1,130]{3,2,1,0:T(1,128)S(1)} %collective-permute-done.23, f32[4,12,1,130]{3,2,1,0:T(1,128)S(1)} %collective-permute-done.22, ...), kind=kLoop, calls=%fused_computation.7 | loop fusion | flops 6291456 | bytes 2466560 | tf_op jit(solution)/shard_map/convert_element_type | solution.py:82
  (88 shorter events, 37.5 us)
Async XLA Ops:
  0.0 9.8 %copy-start.12 = (s32[64,1,2]{0,2,1:T(2,128)S(1)}, s32[64,1,2]{0,2,1:T(2,128)}, u32[]{:S(2)}) copy-start(s32[64,1,2]{0,2,1:T(2,128)} %param.10) | copy-start | bytes 1540
  0.0 10.0 %copy-start.13 = (s32[64,1,2]{0,2,1:T(2,128)S(1)}, s32[64,1,2]{0,2,1:T(2,128)}, u32[]{:S(2)}) copy-start(s32[64,1,2]{0,2,1:T(2,128)} %param.11) | copy-start | bytes 1540
  1.7 23.6 %collective-permute-start = (bf16[48,64,128]{2,0,1:T(8,128)(2,1)S(1)}, bf16[48,64,128]{2,0,1:T(8,128)(2,1)}, u32[]{:S(2)}, u32[]{:S(2)}) collective-permute-start(bf16[48,64,128]{2,0,1:T(8,128)(2,1)S(1)} %copy.39), channel_id=1, source_target_pairs={{0,2},{1,3},{2,4},{3,5},{4,6},{5,7},{6,0},{7,1},{8,10},{9,11},{10,... | collective-permute-start | bytes 2359304 | tf_op jit(solution)/shard_map/ppermute | solution.py:12
  4.8 38.5 %collective-permute-start.1 = (bf16[48,64,128]{2,0,1:T(8,128)(2,1)S(1)}, bf16[48,64,128]{2,0,1:T(8,128)(2,1)S(1)}, u32[]{:S(2)}, u32[]{:S(2)}) collective-permute-start(bf16[48,64,128]{2,0,1:T(8,128)(2,1)S(1)} %copy.39), channel_id=1, source_target_pairs={{0,1},{1,2},{2,3},{3,4},{4,5},{5,6},{6,7},{7,0},{8,9},{9,10},{10,1... | collective-permute-start | bytes 2359304 | tf_op jit(solution)/shard_map/ppermute | solution.py:12
  6.2 39.3 %collective-permute-start.2 = (bf16[48,64,128]{2,0,1:T(8,128)(2,1)S(1)}, bf16[48,64,128]{2,0,1:T(8,128)(2,1)S(1)}, u32[]{:S(2)}, u32[]{:S(2)}) collective-permute-start(bf16[48,64,128]{2,0,1:T(8,128)(2,1)S(1)} %copy.39), channel_id=1, source_target_pairs={{0,7},{1,0},{2,1},{3,2},{4,3},{5,4},{6,5},{7,6},{8,15},{9,8},{10,9... | collective-permute-start | bytes 2359304 | tf_op jit(solution)/shard_map/ppermute | solution.py:12
  9.5 48.5 %collective-permute-start.3 = (bf16[48,64,128]{2,0,1:T(8,128)(2,1)S(1)}, bf16[48,64,128]{2,0,1:T(8,128)(2,1)S(1)}, u32[]{:S(2)}, u32[]{:S(2)}) collective-permute-start(bf16[48,64,128]{2,0,1:T(8,128)(2,1)S(1)} %copy.39), channel_id=1, source_target_pairs={{0,6},{1,7},{2,0},{3,1},{4,2},{5,3},{6,4},{7,5},{8,14},{9,15},{10,... | collective-permute-start | bytes 2359304 | tf_op jit(solution)/shard_map/ppermute | solution.py:12
  10.3 51.6 %copy-start.10 = (pred[128]{0:T(512)(128)(4,1)}, pred[128]{0:T(512)(128)(4,1)S(1)}, u32[]{:S(2)}) copy-start(pred[128]{0:T(512)(128)(4,1)S(1)} %get-tuple-element.6) | copy-start | bytes 388
  10.3 48.6 %copy-start.9 = (s32[1024]{0:T(1024)}, s32[1024]{0:T(1024)S(1)}, u32[]{:S(2)}) copy-start(s32[1024]{0:T(1024)S(1)} %pad_clamp_fusion) | copy-start | bytes 12292
  10.3 33.8 %copy-start.6 = (bf16[4,12,64,128]{3,2,1,0:T(8,128)(2,1)S(1)}, bf16[4,12,64,128]{3,2,1,0:T(8,128)(2,1)}, u32[]{:S(2)}) copy-start(bf16[4,12,64,128]{3,2,1,0:T(8,128)(2,1)} %param.8) | copy-start | bytes 2359300
  65.9 1.0 copy-start.7
  71.1 6.6 %collective-permute-start.4 = (f32[4,12,64,1]{2,0,3,1:T(4,128)S(1)}, f32[4,12,64,1]{2,0,3,1:T(4,128)S(1)}, u32[]{:S(2)}, u32[]{:S(2)}) collective-permute-start(f32[4,12,64,1]{2,0,3,1:T(4,128)S(1)} %copy.45), channel_id=1, source_target_pairs={{0,1},{1,2},{2,3},{3,4},{4,5},{5,6},{6,7},{7,0},{8,9},{9,10},{10,1... | collective-permute-start | bytes 36872 | tf_op jit(solution)/shard_map/ppermute | solution.py:22
  73.8 5.0 %collective-permute-start.5 = (f32[4,12,64,1]{2,0,3,1:T(4,128)}, f32[4,12,64,1]{2,0,3,1:T(4,128)}, u32[]{:S(2)}, u32[]{:S(2)}) collective-permute-start(f32[4,12,64,1]{2,0,3,1:T(4,128)} %copy.46), channel_id=1, source_target_pairs={{1,0},{2,1},{3,2},{4,3},{5,4},{6,5},{7,6},{0,7},{9,8},{10,9},{11,1... | collective-permute-start | bytes 36872 | tf_op jit(solution)/shard_map/ppermute | solution.py:25
  78.3 4.5 %copy-start = (f32[4,12,64,1]{3,2,1,0:T(8,128)}, f32[4,12,64,1]{3,2,1,0:T(8,128)S(1)}, u32[]{:S(2)}) copy-start(f32[4,12,64,1]{3,2,1,0:T(8,128)S(1)} %copy.47) | copy-start | bytes 36868
  81.2 7.7 %copy-start.2 = (f32[4,12,64,1]{3,2,1,0:T(8,128)S(1)}, f32[4,12,64,1]{3,2,1,0:T(8,128)}, u32[]{:S(2)}) copy-start(f32[4,12,64,1]{3,2,1,0:T(8,128)} %copy.48) | copy-start | bytes 36868
  81.2 7.7 %copy-start.8 = (f32[64,128]{1,0:T(8,128)S(1)}, f32[64,128]{1,0:T(8,128)}, u32[]{:S(2)}) copy-start(f32[64,128]{1,0:T(8,128)} %param.13) | copy-start | bytes 98308
  82.8 2.6 %collective-permute-start.6 = (f32[4,12,1,130]{3,2,1,0:T(1,128)S(1)}, f32[4,12,1,130]{3,2,1,0:T(1,128)S(1)}, u32[]{:S(2)}, u32[]{:S(2)}) collective-permute-start(f32[4,12,1,130]{3,2,1,0:T(1,128)S(1)} %get-tuple-element.14), channel_id=1, source_target_pairs={{0,8},{8,16},{16,24},{1,9},{9,17},{17,25},{2,10},{10,18},{18,26},{... | collective-permute-start | bytes 74888 | tf_op jit(solution)/shard_map/ppermute | solution.py:22
  84.1 4.9 %collective-permute-start.7 = (f32[4,12,1,130]{3,2,1,0:T(1,128)S(1)}, f32[4,12,1,130]{3,2,1,0:T(1,128)S(1)}, u32[]{:S(2)}, u32[]{:S(2)}) collective-permute-start(f32[4,12,1,130]{3,2,1,0:T(1,128)S(1)} %get-tuple-element.15), channel_id=1, source_target_pairs={{8,0},{16,8},{24,16},{9,1},{17,9},{25,17},{10,2},{18,10},{26,18},{... | collective-permute-start | bytes 74888 | tf_op jit(solution)/shard_map/ppermute | solution.py:25
  98.3 7.2 %collective-permute-start.8 = (f32[4,12,64,1]{2,0,3,1:T(4,128)}, f32[4,12,64,1]{2,0,3,1:T(4,128)}, u32[]{:S(2)}, u32[]{:S(2)}) collective-permute-start(f32[4,12,64,1]{2,0,3,1:T(4,128)} %copy.51), channel_id=1, source_target_pairs={{0,1},{1,2},{2,3},{3,4},{4,5},{5,6},{6,7},{7,0},{8,9},{9,10},{10,1... | collective-permute-start | bytes 36872 | tf_op jit(solution)/shard_map/ppermute | solution.py:22
  100.1 6.8 %collective-permute-start.9 = (f32[4,12,64,1]{2,0,3,1:T(4,128)}, f32[4,12,64,1]{2,0,3,1:T(4,128)}, u32[]{:S(2)}, u32[]{:S(2)}) collective-permute-start(f32[4,12,64,1]{2,0,3,1:T(4,128)} %copy.52), channel_id=1, source_target_pairs={{1,0},{2,1},{3,2},{4,3},{5,4},{6,5},{7,6},{0,7},{9,8},{10,9},{11,1... | collective-permute-start | bytes 36872 | tf_op jit(solution)/shard_map/ppermute | solution.py:25
  109.4 8.8 %copy-start.3 = (f32[4,12,64,1]{3,2,1,0:T(8,128)S(1)}, f32[4,12,64,1]{3,2,1,0:T(8,128)}, u32[]{:S(2)}) copy-start(f32[4,12,64,1]{3,2,1,0:T(8,128)} %copy.54) | copy-start | bytes 36868
  110.9 5.2 %collective-permute-start.10 = (f32[4,12,1,130]{3,2,1,0:T(1,128)S(1)}, f32[4,12,1,130]{3,2,1,0:T(1,128)S(1)}, u32[]{:S(2)}, u32[]{:S(2)}) collective-permute-start(f32[4,12,1,130]{3,2,1,0:T(1,128)S(1)} %get-tuple-element.12), channel_id=1, source_target_pairs={{0,8},{8,16},{16,24},{1,9},{9,17},{17,25},{2,10},{10,18},{18,26},{... | collective-permute-start | bytes 74888 | tf_op jit(solution)/shard_map/ppermute | solution.py:22
  114.6 3.6 %collective-permute-start.11 = (f32[4,12,1,130]{3,2,1,0:T(1,128)S(1)}, f32[4,12,1,130]{3,2,1,0:T(1,128)S(1)}, u32[]{:S(2)}, u32[]{:S(2)}) collective-permute-start(f32[4,12,1,130]{3,2,1,0:T(1,128)S(1)} %get-tuple-element.13), channel_id=1, source_target_pairs={{8,0},{16,8},{24,16},{9,1},{17,9},{25,17},{10,2},{18,10},{26,18},{... | collective-permute-start | bytes 74888 | tf_op jit(solution)/shard_map/ppermute | solution.py:25
  121.3 20.5 %collective-permute-start.12 = (bf16[48,64,128]{2,0,1:T(8,128)(2,1)S(1)}, bf16[48,64,128]{2,0,1:T(8,128)(2,1)S(1)}, u32[]{:S(2)}, u32[]{:S(2)}) collective-permute-start(bf16[48,64,128]{2,0,1:T(8,128)(2,1)S(1)} %copy.57), channel_id=1, source_target_pairs={{0,2},{1,3},{2,4},{3,5},{4,6},{5,7},{6,0},{7,1},{8,10},{9,11},{10,... | collective-permute-start | bytes 2359304 | tf_op jit(solution)/shard_map/ppermute | solution.py:12
  124.9 36.3 %collective-permute-start.13 = (bf16[48,64,128]{2,0,1:T(8,128)(2,1)S(1)}, bf16[48,64,128]{2,0,1:T(8,128)(2,1)S(1)}, u32[]{:S(2)}, u32[]{:S(2)}) collective-permute-start(bf16[48,64,128]{2,0,1:T(8,128)(2,1)S(1)} %copy.57), channel_id=1, source_target_pairs={{0,1},{1,2},{2,3},{3,4},{4,5},{5,6},{6,7},{7,0},{8,9},{9,10},{10,1... | collective-permute-start | bytes 2359304 | tf_op jit(solution)/shard_map/ppermute | solution.py:12
  125.9 37.6 %collective-permute-start.14 = (bf16[48,64,128]{2,0,1:T(8,128)(2,1)S(1)}, bf16[48,64,128]{2,0,1:T(8,128)(2,1)S(1)}, u32[]{:S(2)}, u32[]{:S(2)}) collective-permute-start(bf16[48,64,128]{2,0,1:T(8,128)(2,1)S(1)} %copy.57), channel_id=1, source_target_pairs={{0,7},{1,0},{2,1},{3,2},{4,3},{5,4},{6,5},{7,6},{8,15},{9,8},{10,9... | collective-permute-start | bytes 2359304 | tf_op jit(solution)/shard_map/ppermute | solution.py:12
  129.6 47.7 %collective-permute-start.15 = (bf16[48,64,128]{2,0,1:T(8,128)(2,1)S(1)}, bf16[48,64,128]{2,0,1:T(8,128)(2,1)S(1)}, u32[]{:S(2)}, u32[]{:S(2)}) collective-permute-start(bf16[48,64,128]{2,0,1:T(8,128)(2,1)S(1)} %copy.57), channel_id=1, source_target_pairs={{0,6},{1,7},{2,0},{3,1},{4,2},{5,3},{6,4},{7,5},{8,14},{9,15},{10,... | collective-permute-start | bytes 2359304 | tf_op jit(solution)/shard_map/ppermute | solution.py:12
  178.2 3.1 %copy-start.11 = (pred[128]{0:T(512)(128)(4,1)S(1)}, pred[128]{0:T(512)(128)(4,1)}, u32[]{:S(2)}) copy-start(pred[128]{0:T(512)(128)(4,1)} %copy-done.10) | copy-start | bytes 388
  190.1 6.6 %collective-permute-start.16 = (f32[4,12,64,1]{2,0,3,1:T(4,128)S(1)}, f32[4,12,64,1]{2,0,3,1:T(4,128)S(1)}, u32[]{:S(2)}, u32[]{:S(2)}) collective-permute-start(f32[4,12,64,1]{2,0,3,1:T(4,128)S(1)} %copy.63), channel_id=1, source_target_pairs={{0,1},{1,2},{2,3},{3,4},{4,5},{5,6},{6,7},{7,0},{8,9},{9,10},{10,1... | collective-permute-start | bytes 36872 | tf_op jit(solution)/shard_map/ppermute | solution.py:22
  193.5 3.9 %collective-permute-start.17 = (f32[4,12,64,1]{2,0,3,1:T(4,128)S(1)}, f32[4,12,64,1]{2,0,3,1:T(4,128)S(1)}, u32[]{:S(2)}, u32[]{:S(2)}) collective-permute-start(f32[4,12,64,1]{2,0,3,1:T(4,128)S(1)} %copy.64), channel_id=1, source_target_pairs={{1,0},{2,1},{3,2},{4,3},{5,4},{6,5},{7,6},{0,7},{9,8},{10,9},{11,1... | collective-permute-start | bytes 36872 | tf_op jit(solution)/shard_map/ppermute | solution.py:25
  197.2 3.4 %copy-start.1 = (f32[4,12,64,1]{3,2,1,0:T(8,128)}, f32[4,12,64,1]{3,2,1,0:T(8,128)S(1)}, u32[]{:S(2)}) copy-start(f32[4,12,64,1]{3,2,1,0:T(8,128)S(1)} %copy.65) | copy-start | bytes 36868
  199.0 6.0 %copy-start.4 = (f32[4,12,64,1]{3,2,1,0:T(8,128)S(1)}, f32[4,12,64,1]{3,2,1,0:T(8,128)}, u32[]{:S(2)}) copy-start(f32[4,12,64,1]{3,2,1,0:T(8,128)} %copy.66) | copy-start | bytes 36868
  200.6 2.6 %collective-permute-start.18 = (f32[4,12,1,130]{3,2,1,0:T(1,128)S(1)}, f32[4,12,1,130]{3,2,1,0:T(1,128)S(1)}, u32[]{:S(2)}, u32[]{:S(2)}) collective-permute-start(f32[4,12,1,130]{3,2,1,0:T(1,128)S(1)} %get-tuple-element.10), channel_id=1, source_target_pairs={{0,8},{8,16},{16,24},{1,9},{9,17},{17,25},{2,10},{10,18},{18,26},{... | collective-permute-start | bytes 74888 | tf_op jit(solution)/shard_map/ppermute | solution.py:22
  201.9 3.1 %collective-permute-start.19 = (f32[4,12,1,130]{3,2,1,0:T(1,128)S(1)}, f32[4,12,1,130]{3,2,1,0:T(1,128)S(1)}, u32[]{:S(2)}, u32[]{:S(2)}) collective-permute-start(f32[4,12,1,130]{3,2,1,0:T(1,128)S(1)} %get-tuple-element.11), channel_id=1, source_target_pairs={{8,0},{16,8},{24,16},{9,1},{17,9},{25,17},{10,2},{18,10},{26,18},{... | collective-permute-start | bytes 74888 | tf_op jit(solution)/shard_map/ppermute | solution.py:25
  213.8 6.6 %collective-permute-start.20 = (f32[4,12,64,1]{2,0,3,1:T(4,128)S(1)}, f32[4,12,64,1]{2,0,3,1:T(4,128)S(1)}, u32[]{:S(2)}, u32[]{:S(2)}) collective-permute-start(f32[4,12,64,1]{2,0,3,1:T(4,128)S(1)} %copy.69), channel_id=1, source_target_pairs={{0,1},{1,2},{2,3},{3,4},{4,5},{5,6},{6,7},{7,0},{8,9},{9,10},{10,1... | collective-permute-start | bytes 36872 | tf_op jit(solution)/shard_map/ppermute | solution.py:22
  215.2 6.3 %collective-permute-start.21 = (f32[4,12,64,1]{2,0,3,1:T(4,128)S(1)}, f32[4,12,64,1]{2,0,3,1:T(4,128)S(1)}, u32[]{:S(2)}, u32[]{:S(2)}) collective-permute-start(f32[4,12,64,1]{2,0,3,1:T(4,128)S(1)} %copy.70), channel_id=1, source_target_pairs={{1,0},{2,1},{3,2},{4,3},{5,4},{6,5},{7,6},{0,7},{9,8},{10,9},{11,1... | collective-permute-start | bytes 36872 | tf_op jit(solution)/shard_map/ppermute | solution.py:25
  223.3 8.8 %copy-start.5 = (f32[4,12,64,1]{3,2,1,0:T(8,128)S(1)}, f32[4,12,64,1]{3,2,1,0:T(8,128)}, u32[]{:S(2)}) copy-start(f32[4,12,64,1]{3,2,1,0:T(8,128)} %copy.72) | copy-start | bytes 36868
  224.8 4.8 %collective-permute-start.22 = (f32[4,12,1,130]{3,2,1,0:T(1,128)S(1)}, f32[4,12,1,130]{3,2,1,0:T(1,128)S(1)}, u32[]{:S(2)}, u32[]{:S(2)}) collective-permute-start(f32[4,12,1,130]{3,2,1,0:T(1,128)S(1)} %get-tuple-element.8), channel_id=1, source_target_pairs={{0,8},{8,16},{16,24},{1,9},{9,17},{17,25},{2,10},{10,18},{18,26},{... | collective-permute-start | bytes 74888 | tf_op jit(solution)/shard_map/ppermute | solution.py:22
  228.3 3.8 %collective-permute-start.23 = (f32[4,12,1,130]{3,2,1,0:T(1,128)S(1)}, f32[4,12,1,130]{3,2,1,0:T(1,128)S(1)}, u32[]{:S(2)}, u32[]{:S(2)}) collective-permute-start(f32[4,12,1,130]{3,2,1,0:T(1,128)S(1)} %get-tuple-element.9), channel_id=1, source_target_pairs={{8,0},{16,8},{24,16},{9,1},{17,9},{25,17},{10,2},{18,10},{26,18},{... | collective-permute-start | bytes 74888 | tf_op jit(solution)/shard_map/ppermute | solution.py:25
where the time goes:
time: 240 us; the launch traced here: 235 us
  waiting for transfers between devices  101 us (42%)
  local copies, waits for them, and re-layouts  51.7 us (22%)
  starting transfers between devices  51 us (21%)
  other arithmetic  23.6 us (10%)
  matrix products  7.47 us (3%)
    ppermute x8, waiting for transfers between devices, passed_along(): return lax.ppermute(x, axis, [(i, (i + by) % size) for i in range(size)])  85.8 us
    ppermute x8, starting transfers between devices, padded(): lax.ppermute(lax.slice_in_dim(block, 0, width, axis=dim), axis, backward)  18.8 us
    ppermute x8, starting transfers between devices, passed_along(): return lax.ppermute(x, axis, [(i, (i + by) % size) for i in range(size)])  16.4 us
    ppermute x8, starting transfers between devices, padded(): lax.ppermute(lax.slice_in_dim(block, block.shape[dim] - width, None, axis...  15.9 us
    slice x8, local copies, waits for them, and re-layouts, padded(): lax.slice_in_dim(block, block.shape[dim] - width, None, axis=dim)  15.4 us
    ppermute x8, waiting for transfers between devices, padded(): lax.ppermute(lax.slice_in_dim(block, 0, width, axis=dim), axis, backward)  11.3 us
    add x2, other arithmetic, relax(): return center + coef * (beside_all - 4.0 * center)  10.1 us
    unnamed x36, local copies, waits for them, and re-layouts  10.1 us
  transfers between devices with their start and end apart: 24, of which 18 were waited for; matrix products, arithmetic and copies ran while one was open for 7% of the time, Pallas kernels for 0%

commit v1 on v0

v1 whole, which is shorter than its diff:
```python
import functools

import jax
import jax.numpy as jnp
from jax import lax
from jax.experimental import pallas as pl
from jax.experimental.pallas import tpu as pltpu
from jax.sharding import PartitionSpec as P

STEPS = 2
SUBSTEPS = 2
OFFSETS = (-2, -1, 1, 2)
CAP = 32
MESH = pl.DeviceIdType.MESH
CONTRACT_LAST = (((1,), (1,)), ((), ()))
CONTRACT_FIRST = (((0,), (0,)), ((), ()))


def one_hot(rows, row, lane):
    at_row = lax.broadcasted_iota(jnp.int32, (rows, 128), 0) == row
    at_lane = lax.broadcasted_iota(jnp.int32, (rows, 128), 1) == lane
    return jnp.where(at_row & at_lane, 1.0, 0.0)


def kernel(
    n_lat, n_lon,
    pick_ref, list_ref, field_ref, weights_ref, kv_ref, kh_ref, out_ref,
    weights_buf, asked, asked_smem, blocks_first, blocks_second, field_second, packed, h, x_halo, edge, edge_in,
    weights_sem, list_send, list_recv, list_local, block_send, block_recv,
    row_send, row_recv, edge_send, edge_recv,
):
    lat, lon = lax.axis_index("lat"), lax.axis_index("lon")
    tile_rows, channels, _ = field_ref.shape
    group = tile_rows // 4

    def sector(by):
        return lax.rem(lon + by + n_lon, n_lon)

    weights_copy = pltpu.make_async_copy(weights_ref, weights_buf, weights_sem)
    weights_copy.start()
    for step in range(STEPS):
        for sub in range(SUBSTEPS):
            h[step, sub, 0] = jnp.zeros_like(h[step, sub, 0])
            h[step, sub, tile_rows + 1] = jnp.zeros_like(h[step, sub, 0])

    barrier = pltpu.get_barrier_semaphore()
    for by in OFFSETS:
        pl.semaphore_signal(barrier, 1, device_id=(lat, sector(by)), device_id_type=MESH)

    @pl.when(lat > 0)
    def _():
        pl.semaphore_signal(barrier, 1, device_id=(lat - 1, lon), device_id_type=MESH)

    @pl.when(lat < n_lat - 1)
    def _():
        pl.semaphore_signal(barrier, 1, device_id=(lat + 1, lon), device_id_type=MESH)

    own_blocks = len(OFFSETS) * CAP
    blocks_of, field_of = (blocks_first, blocks_second), (field_ref, field_second)
    inner = jnp.where(lat > 0, 1, 0) + jnp.where(lat < n_lat - 1, 1, 0)
    pl.semaphore_wait(barrier, len(OFFSETS) + inner)

    list_copies = []
    for i, by in enumerate(OFFSETS):
        copy = pltpu.make_async_remote_copy(
            src_ref=list_ref.at[i], dst_ref=asked.at[i],
            send_sem=list_send.at[i], recv_sem=list_recv.at[i],
            device_id=(lat, sector(by)), device_id_type=MESH,
        )
        copy.start()
        list_copies.append(copy)

    def own(r, carry):
        blocks_first[own_blocks + r] = field_ref[r]
        return carry

    lax.fori_loop(0, tile_rows, own, 0, unroll=8)
    for copy in list_copies:
        copy.wait()
    local = pltpu.make_async_copy(asked, asked_smem, list_local)
    local.start()
    local.wait()

    lane = lax.broadcasted_iota(jnp.int32, (channels, 128), 1)

    for step in range(STEPS):
        block_copies, blocks, field = [], blocks_of[step], field_of[step]
        for i, by in enumerate(OFFSETS):
            def pack(s, carry, i=i):
                packed[step, i * CAP + s] = field[asked_smem[i, 0, s]]
                return carry

            lax.fori_loop(0, CAP, pack, 0, unroll=8)
            here = pl.ds(i * CAP, CAP)
            copy = pltpu.make_async_remote_copy(
                src_ref=packed.at[step, here], dst_ref=blocks.at[here],
                send_sem=block_send.at[step, i], recv_sem=block_recv.at[step, i],
                device_id=(lat, sector(-by)), device_id_type=MESH,
            )
            copy.start()
            block_copies.append(copy)
        if step == 0:
            weights_copy.wait()
        for copy in block_copies:
            copy.wait()

        def advect(y, carry):
            source = jnp.concatenate(
                [blocks[pick_ref[2 * y]], blocks[pick_ref[2 * y + 1]]], axis=1
            )
            remap = jnp.concatenate([weights_buf[y, 0], weights_buf[y, 1]], axis=1)
            advected = lax.dot_general(
                source, remap, CONTRACT_LAST, preferred_element_type=jnp.float32
            )
            flux = kv_ref[y] * (pltpu.roll(advected, channels - 1, 0) - advected)
            h[step, 0, 1 + y] = advected + flux - pltpu.roll(flux, 1, 0)
            return carry

        lax.fori_loop(0, tile_rows, advect, 0, unroll=4)

        for sub in range(SUBSTEPS):
            now = h.at[step, sub]
            up = pltpu.make_async_remote_copy(
                src_ref=now.at[1], dst_ref=now.at[tile_rows + 1],
                send_sem=row_send.at[step, sub, 0], recv_sem=row_recv.at[step, sub, 0],
                device_id=(lat - 1, lon), device_id_type=MESH,
            )
            down = pltpu.make_async_remote_copy(
                src_ref=now.at[tile_rows], dst_ref=now.at[0],
                send_sem=row_send.at[step, sub, 1], recv_sem=row_recv.at[step, sub, 1],
                device_id=(lat + 1, lon), device_id_type=MESH,
            )

            @pl.when(lat > 0)
            def _():
                up.start()

            @pl.when(lat < n_lat - 1)
            def _():
                down.start()

            total = None
            for g in range(4):
                rows = now[pl.ds(1 + g * group, group)].reshape(group * channels, 128)
                choose = one_hot(8, 2 * g, 0) + one_hot(8, 2 * g + 1, 127)
                part = lax.dot_general(
                    choose.astype(jnp.bfloat16), rows.astype(jnp.bfloat16), CONTRACT_LAST,
                    preferred_element_type=jnp.float32,
                )
                total = part if total is None else total + part
            edge[step, sub] = total
            edge_copies = []
            for i, by in enumerate((1, -1)):
                copy = pltpu.make_async_remote_copy(
                    src_ref=edge.at[step, sub], dst_ref=edge_in.at[step, sub, i],
                    send_sem=edge_send.at[step, sub, i], recv_sem=edge_recv.at[step, sub, i],
                    device_id=(lat, sector(by)), device_id_type=MESH,
                )
                copy.start()
                edge_copies.append(copy)
            for copy in edge_copies:
                copy.wait()
            beside = edge_in[step, sub].reshape(16, group * channels).astype(jnp.bfloat16)
            for g in range(4):
                place = one_hot(16, 2 * g + 1, 127) + one_hot(16, 8 + 2 * g, 0)
                part = lax.dot_general(
                    beside, place.astype(jnp.bfloat16), CONTRACT_FIRST,
                    preferred_element_type=jnp.float32,
                )
                x_halo[pl.ds(g * group, group)] = part.reshape(group, channels, 128)

            @pl.when(lat > 0)
            def _():
                up.wait_send()
                down.wait_recv()

            @pl.when(lat < n_lat - 1)
            def _():
                down.wait_send()
                up.wait_recv()

            def relax(y, carry):
                center = now[1 + y]
                halo = x_halo[y]
                west = pltpu.roll(jnp.where(lane == 127, halo, center), 1, 1)
                east = pltpu.roll(jnp.where(lane == 0, halo, center), 127, 1)
                beside_all = now[y] + now[2 + y] + west + east
                new = center + kh_ref[pl.ds(y, 1)] * (beside_all - 4.0 * center)
                if sub < SUBSTEPS - 1:
                    h[step, sub + 1, 1 + y] = new
                elif step < STEPS - 1:
                    field_second[y] = new.astype(jnp.bfloat16)
                    blocks_second[own_blocks + y] = new.astype(jnp.bfloat16)
                else:
                    out_ref[y] = new.astype(jnp.bfloat16)
                return carry

            lax.fori_loop(0, tile_rows, relax, 0, unroll=4)


def local(n_lat, n_lon, tracers, weights, src_row, src_sector, kv, kh):
    tracer_count, level_count, tile_rows, tile_cols = tracers.shape
    channels = tracer_count * level_count
    reach = src_row.shape[2]
    requests = tile_rows * reach
    row = src_row.reshape(requests) - lax.axis_index("lat") * tile_rows
    nearby = (src_sector.reshape(requests) - lax.axis_index("lon") + 2 + n_lon) % n_lon
    order = jnp.arange(requests, dtype=jnp.int32)
    earlier = (nearby[:, None] == nearby[None]) & (order[None] < order[:, None])
    rank = jnp.sum(earlier, axis=1, dtype=jnp.int32)
    slot = jnp.where(nearby > 2, nearby - 1, nearby) * CAP + rank
    pick = jnp.where(nearby == 2, len(OFFSETS) * CAP + row, slot).astype(jnp.int32)
    places = jnp.arange(len(OFFSETS) * CAP, dtype=jnp.int32)
    taken = places[:, None] == jnp.where(nearby == 2, -1, slot)[None]
    lists = jnp.sum(jnp.where(taken, row[None], 0), axis=1, dtype=jnp.int32)
    lists = jnp.pad(lists.reshape(len(OFFSETS), 1, CAP), ((0, 0), (0, 7), (0, 128 - CAP)))

    field = tracers.reshape(channels, tile_rows, tile_cols).transpose(1, 0, 2)
    kv_all = jnp.pad(kv, ((0, 1), (0, 0), (0, 0))).transpose(1, 0, 2)
    kv_all = jnp.tile(kv_all, (1, tracer_count, 1))
    bf16, f32, i32 = jnp.bfloat16, jnp.float32, jnp.int32
    vmem = pl.BlockSpec(memory_space=pltpu.VMEM)
    smem = pl.BlockSpec(memory_space=pltpu.SMEM)
    count = len(OFFSETS)
    edge_shape = (8, tile_rows // 4 * channels)
    dma = pltpu.SemaphoreType.DMA
    out = pl.pallas_call(
        functools.partial(kernel, n_lat, n_lon),
        out_shape=jax.ShapeDtypeStruct(field.shape, bf16),
        in_specs=[smem, vmem, vmem, pl.BlockSpec(memory_space=pl.ANY), vmem, vmem],
        out_specs=vmem,
        scratch_shapes=[
            pltpu.VMEM(weights.shape, bf16),
            pltpu.VMEM((count, 8, 128), i32),
            pltpu.SMEM((count, 8, 128), i32),
            pltpu.VMEM((count * CAP + tile_rows, channels, tile_cols), bf16),
            pltpu.VMEM((count * CAP + tile_rows, channels, tile_cols), bf16),
            pltpu.VMEM(field.shape, bf16),
            pltpu.VMEM((STEPS, count * CAP, channels, tile_cols), bf16),
            pltpu.VMEM((STEPS, SUBSTEPS, tile_rows + 2, channels, tile_cols), f32),
            pltpu.VMEM((tile_rows, channels, tile_cols), f32),
            pltpu.VMEM((STEPS, SUBSTEPS) + edge_shape, f32),
            pltpu.VMEM((STEPS, SUBSTEPS, 2) + edge_shape, f32),
            dma, dma((count,)), dma((count,)), dma,
            dma((STEPS, count)), dma((STEPS, count)),
            dma((STEPS, SUBSTEPS, 2)), dma((STEPS, SUBSTEPS, 2)),
            dma((STEPS, SUBSTEPS, 2)), dma((STEPS, SUBSTEPS, 2)),
        ],
        compiler_params=pltpu.CompilerParams(
            collective_id=0, has_side_effects=True, vmem_limit_bytes=44 * 1024 * 1024
        ),
    )(pick, lists, field, weights, kv_all, kh)
    return out.transpose(1, 0, 2).reshape(tracers.shape)


def solution(mesh):
    return jax.shard_map(
        functools.partial(local, mesh.shape["lat"], mesh.shape["lon"]),
        mesh=mesh,
        in_specs=(
            P(None, None, "lat", "lon"),
            P("lat", None, "lon", None),
            P("lat", "lon", None),
            P("lat", "lon", None),
            P(None, "lat", "lon"),
            P("lat", "lon"),
        ),
        out_specs=P(None, None, "lat", "lon"),
        check_vma=False,
    )
```

time: 240 us -> 105 us (0.44); the launches traced: 235 us -> 105 us
  waiting for transfers between devices: 101 us -> 0 us
  Pallas kernels: 0 us -> 98 us
  starting transfers between devices: 51 us -> 0 us
  local copies, waits for them, and re-layouts: 51.7 us -> 5.11 us
  other arithmetic: 23.6 us -> 1.67 us
  matrix products: 7.47 us -> 0 us
    ppermute x24 -> x0, waiting for transfers between devices: 101 us -> none  [the longest x8 85.8 us: passed_along(): return lax.ppermute(x, axis, [(i, (i + by) % size) for i in range(size)])]
    pallas_call x0 -> x1, Pallas kernels: none -> 98 us  [local(): pl.pallas_call(functools.partial(kernel, n_lat, n_lon), out_shape=jax.Sha...]
    ppermute x24 -> x0, starting transfers between devices: 51 us -> none  [the longest x8 18.8 us: padded(): lax.ppermute(lax.slice_in_dim(block, 0, width, axis=dim), axis, backward)]
    slice x12 -> x0, local copies, waits for them, and re-layouts: 18.7 us -> none  [the longest x8 15.4 us: padded(): lax.slice_in_dim(block, block.shape[dim] - width, None, axis=dim)]
    ppermute x8 -> x0, local copies, waits for them, and re-layouts: 11.3 us -> none  [the longest x4 8.39 us: padded(): lax.ppermute(lax.slice_in_dim(block, 0, width, axis=dim), axis, backward)]
    add x3 -> x1, other arithmetic: 10.1 us -> 0.68 us  [local(): src_sector.reshape(requests) - lax.axis_index('lon') + 2 + n_lon]
    unnamed x36 -> x6, local copies, waits for them, and re-layouts: 10.1 us -> 0.83 us
    dot_general x2 -> x0, matrix products: 7.47 us -> none  [local(): jnp.einsum('cykq,ykpq->cyp', source, weights, preferred_element_type=jnp....]
  transfers between devices with their start and end apart: 24 -> 0, of which waited for: 18 -> 0; matrix products, arithmetic and copies ran while one was open for 7% -> 0% of each run, Pallas kernels for 0% -> 0%
where the time goes in v1:
time: 105 us
  Pallas kernels  98 us (93%)
  local copies, waits for them, and re-layouts  5.11 us (5%)
  other arithmetic  1.67 us (2%)
    pallas_call x1, Pallas kernels, local(): pl.pallas_call(functools.partial(kernel, n_lat, n_lon), out_shape=jax.Sha...  98 us

profile of v1, /device:TPU:0, one launch (start us, length us, event | category | flops | bytes accessed | tf_op | source)
XLA Modules:
  0.0 104.9 jit_solution(5282477055046305514)
XLA Ops:
  0.0 0.7 subtract_add_fusion
  0.7 0.1 copy.19
  0.8 0.1 add.64
  0.9 0.2 convert_reduce_fusion
  1.1 0.7 broadcast_subtract_fusion
  1.8 0.1 copy.20
  1.9 0.1 sub.39
  2.1 0.1 select_reduce_fusion
  2.2 0.1 reshape.72
  2.3 1.0 pad_bitcast_fusion
  3.3 0.0 copy-start.2
  3.3 0.2 tile.4
  3.5 0.0 copy-start
  3.5 0.9 copy.23.kv_ref
  4.4 0.0 copy-start.1
  4.4 0.0 copy-done.2
  4.5 0.5 copy.26
  5.0 0.8 copy-done
  5.8 0.0 copy-done.1
  5.8 98.0 %shard_map.64 = bf16[64,48,128]{2,1,0:T(8,128)(2,1)S(1)} custom-call(s32[128]{0:T(128)S(1)} %get-tuple-element.6.pick_ref, s32[4,8,128]{2,1,0:T(8,128)S(1)} %pad.8.list_ref, bf16[64,48,128]{2,1,0:T(8,128)(2,1)S(1)} %bitcast.15, bf16[64,2,128,128]{3,2,1,0:T(8,128)(2,1)S(1)} %copy-done, f32[64,48,128]{2,1,0:T(8,128)S(1)} %copy.23.kv_ref, f32[64,128]{1,0:T(8,128)S(1)} %copy-done.1), custom_call_target="tpu_custom_call" | custom-call | tf_op jit(solution)/shard_map/pallas_call | solution.py:227
  103.8 1.1 %copy.24 = bf16[48,64,128]{2,1,0:T(8,128)(2,1)} copy(bf16[48,64,128]{2,0,1:T(8,128)(2,1)S(1)} %bitcast.14) | data formatting | bytes 1572864 | tf_op jit(solution)/shard_map/transpose | solution.py:253
  (3 shorter events, 0.0 us)
Async XLA Ops:
  3.3 1.1 %copy-start.2 = (bf16[4,12,64,128]{3,2,1,0:T(8,128)(2,1)S(1)}, bf16[4,12,64,128]{3,2,1,0:T(8,128)(2,1)}, u32[]{:S(2)}) copy-start(bf16[4,12,64,128]{3,2,1,0:T(8,128)(2,1)} %param.6) | copy-start | bytes 2359300
  3.5 2.3 %copy-start = (bf16[64,2,128,128]{3,2,1,0:T(8,128)(2,1)S(1)}, bf16[64,2,128,128]{3,2,1,0:T(8,128)(2,1)}, u32[]{:S(2)}) copy-start(bf16[64,2,128,128]{3,2,1,0:T(8,128)(2,1)} %weights_ref.1) | copy-start | bytes 12582916
  4.4 1.4 %copy-start.1 = (f32[64,128]{1,0:T(8,128)S(1)}, f32[64,128]{1,0:T(8,128)}, u32[]{:S(2)}) copy-start(f32[64,128]{1,0:T(8,128)} %kh_ref.1) | copy-start | bytes 98308

commit v2 on v1

v2 whole, which is shorter than its diff:
```python
import functools

import jax
import jax.numpy as jnp
from jax import lax
from jax.experimental import pallas as pl
from jax.experimental.pallas import tpu as pltpu
from jax.sharding import PartitionSpec as P

STEPS = 2
SUBSTEPS = 2
OFFSETS = (-2, -1, 1, 2)
CAP = 32
GROUPS = 2
CUTS = (0, 8, 20, 32)
MESH = pl.DeviceIdType.MESH
CONTRACT_LAST = (((1,), (1,)), ((), ()))
CONTRACT_FIRST = (((0,), (0,)), ((), ()))


def one_hot(rows, row, lane):
    at_row = lax.broadcasted_iota(jnp.int32, (rows, 128), 0) == row
    at_lane = lax.broadcasted_iota(jnp.int32, (rows, 128), 1) == lane
    return jnp.where(at_row & at_lane, 1.0, 0.0)


def kernel(
    n_lat, n_lon,
    pick_ref, list_ref, field_ref, weights_ref, kv_ref, kh_ref, out_ref,
    weights_buf, asked, asked_smem, blocks_a, blocks_b, blocks_c, blocks_d, field_second, packed, h, x_halo, edge, edge_in,
    weights_sem, list_send, list_recv, list_local, block_send, block_recv,
    row_send, row_recv, edge_send, edge_recv,
):
    lat, lon = lax.axis_index("lat"), lax.axis_index("lon")
    _, tile_rows, channels, _ = field_ref.shape
    group = tile_rows // 4

    def sector(by):
        return lax.rem(lon + by + n_lon, n_lon)

    weights_copy = pltpu.make_async_copy(weights_ref, weights_buf, weights_sem)
    weights_copy.start()
    for turn in range(STEPS * GROUPS):
        for sub in range(SUBSTEPS):
            h[turn, sub, 0] = jnp.zeros_like(h[turn, sub, 0])
            h[turn, sub, tile_rows + 1] = jnp.zeros_like(h[turn, sub, 0])

    barrier = pltpu.get_barrier_semaphore()
    for by in OFFSETS:
        pl.semaphore_signal(barrier, 1, device_id=(lat, sector(by)), device_id_type=MESH)

    @pl.when(lat > 0)
    def _():
        pl.semaphore_signal(barrier, 1, device_id=(lat - 1, lon), device_id_type=MESH)

    @pl.when(lat < n_lat - 1)
    def _():
        pl.semaphore_signal(barrier, 1, device_id=(lat + 1, lon), device_id_type=MESH)

    own_blocks = len(OFFSETS) * CAP
    blocks_of, field_of = (blocks_a, blocks_b, blocks_c, blocks_d), (field_ref, field_second)
    inner = jnp.where(lat > 0, 1, 0) + jnp.where(lat < n_lat - 1, 1, 0)
    pl.semaphore_wait(barrier, len(OFFSETS) + inner)

    list_copies = []
    for i, by in enumerate(OFFSETS):
        copy = pltpu.make_async_remote_copy(
            src_ref=list_ref.at[i], dst_ref=asked.at[i],
            send_sem=list_send.at[i], recv_sem=list_recv.at[i],
            device_id=(lat, sector(by)), device_id_type=MESH,
        )
        copy.start()
        list_copies.append(copy)

    def own(r, carry):
        for part in range(GROUPS):
            blocks_of[part][own_blocks + r] = field_ref[part, r]
        return carry

    lax.fori_loop(0, tile_rows, own, 0, unroll=8)
    for copy in list_copies:
        copy.wait()
    local = pltpu.make_async_copy(asked, asked_smem, list_local)
    local.start()
    local.wait()

    lane = lax.broadcasted_iota(jnp.int32, (channels, 128), 1)

    def send_blocks(turn, cut):
        step, part = divmod(turn, GROUPS)
        first, count = CUTS[cut], CUTS[cut + 1] - CUTS[cut]
        field, copies = field_of[step], []
        for i, by in enumerate(OFFSETS):
            def pack(s, carry, i=i):
                packed[turn, i * CAP + s] = field[part, asked_smem[i, 0, s]]
                return carry

            lax.fori_loop(first, first + count, pack, 0, unroll=4)
            here = pl.ds(i * CAP + first, count)
            copy = pltpu.make_async_remote_copy(
                src_ref=packed.at[turn, here], dst_ref=blocks_of[turn].at[here],
                send_sem=block_send.at[turn, cut, i], recv_sem=block_recv.at[turn, cut, i],
                device_id=(lat, sector(-by)), device_id_type=MESH,
            )
            copy.start()
            copies.append(copy)
        return copies

    cuts = len(CUTS) - 1
    block_copies = [[] for _ in range(STEPS * GROUPS)]
    for cut in range(cuts):
        block_copies[0] += send_blocks(0, cut)
    weights_copy.wait()

    for turn in range(STEPS * GROUPS):
        step, part = divmod(turn, GROUPS)
        blocks = blocks_of[turn]
        for copy in block_copies[turn]:
            copy.wait()
        if turn + 1 < STEPS * GROUPS:
            block_copies[turn + 1] += send_blocks(turn + 1, 0)

        def advect(y, carry):
            source = jnp.concatenate(
                [blocks[pick_ref[2 * y]], blocks[pick_ref[2 * y + 1]]], axis=1
            )
            remap = jnp.concatenate([weights_buf[y, 0], weights_buf[y, 1]], axis=1)
            advected = lax.dot_general(
                source, remap, CONTRACT_LAST, preferred_element_type=jnp.float32
            )
            flux = kv_ref[y] * (pltpu.roll(advected, channels - 1, 0) - advected)
            h[turn, 0, 1 + y] = advected + flux - pltpu.roll(flux, 1, 0)
            return carry

        lax.fori_loop(0, tile_rows, advect, 0, unroll=16)

        for sub in range(SUBSTEPS):
            now = h.at[turn, sub]
            up = pltpu.make_async_remote_copy(
                src_ref=now.at[1], dst_ref=now.at[tile_rows + 1],
                send_sem=row_send.at[turn, sub, 0], recv_sem=row_recv.at[turn, sub, 0],
                device_id=(lat - 1, lon), device_id_type=MESH,
            )
            down = pltpu.make_async_remote_copy(
                src_ref=now.at[tile_rows], dst_ref=now.at[0],
                send_sem=row_send.at[turn, sub, 1], recv_sem=row_recv.at[turn, sub, 1],
                device_id=(lat + 1, lon), device_id_type=MESH,
            )

            @pl.when(lat > 0)
            def _():
                up.start()

            @pl.when(lat < n_lat - 1)
            def _():
                down.start()

            total = None
            for g in range(4):
                rows = now[pl.ds(1 + g * group, group)].reshape(group * channels, 128)
                choose = one_hot(8, 2 * g, 0) + one_hot(8, 2 * g + 1, 127)
                piece = lax.dot_general(
                    choose.astype(jnp.bfloat16), rows.astype(jnp.bfloat16), CONTRACT_LAST,
                    preferred_element_type=jnp.float32,
                )
                total = piece if total is None else total + piece
            edge[turn, sub] = total
            edge_copies = []
            for i, by in enumerate((1, -1)):
                copy = pltpu.make_async_remote_copy(
                    src_ref=edge.at[turn, sub], dst_ref=edge_in.at[turn, sub, i],
                    send_sem=edge_send.at[turn, sub, i], recv_sem=edge_recv.at[turn, sub, i],
                    device_id=(lat, sector(by)), device_id_type=MESH,
                )
                copy.start()
                edge_copies.append(copy)
            if turn + 1 < STEPS * GROUPS:
                block_copies[turn + 1] += send_blocks(turn + 1, 1 + sub)
            for copy in edge_copies:
                copy.wait()
            beside = edge_in[turn, sub].reshape(16, group * channels).astype(jnp.bfloat16)
            for g in range(4):
                place = one_hot(16, 2 * g + 1, 127) + one_hot(16, 8 + 2 * g, 0)
                piece = lax.dot_general(
                    beside, place.astype(jnp.bfloat16), CONTRACT_FIRST,
                    preferred_element_type=jnp.float32,
                )
                x_halo[pl.ds(g * group, group)] = piece.reshape(group, channels, 128)

            @pl.when(lat > 0)
            def _():
                up.wait_send()
                down.wait_recv()

            @pl.when(lat < n_lat - 1)
            def _():
                down.wait_send()
                up.wait_recv()

            def relax(y, carry):
                center = now[1 + y]
                halo = x_halo[y]
                west = pltpu.roll(jnp.where(lane == 127, halo, center), 1, 1)
                east = pltpu.roll(jnp.where(lane == 0, halo, center), 127, 1)
                beside_all = now[y] + now[2 + y] + west + east
                new = center + kh_ref[pl.ds(y, 1)] * (beside_all - 4.0 * center)
                if sub < SUBSTEPS - 1:
                    h[turn, sub + 1, 1 + y] = new
                elif step < STEPS - 1:
                    field_second[part, y] = new.astype(jnp.bfloat16)
                    blocks_of[GROUPS + part][own_blocks + y] = new.astype(jnp.bfloat16)
                else:
                    out_ref[part, y] = new.astype(jnp.bfloat16)
                return carry

            lax.fori_loop(0, tile_rows, relax, 0, unroll=16)


def local(n_lat, n_lon, tracers, weights, src_row, src_sector, kv, kh):
    tracer_count, level_count, tile_rows, tile_cols = tracers.shape
    channels = tracer_count // GROUPS * level_count
    reach = src_row.shape[2]
    requests = tile_rows * reach
    row = src_row.reshape(requests) - lax.axis_index("lat") * tile_rows
    nearby = (src_sector.reshape(requests) - lax.axis_index("lon") + 2 + n_lon) % n_lon
    order = jnp.arange(requests, dtype=jnp.int32)
    earlier = (nearby[:, None] == nearby[None]) & (order[None] < order[:, None])
    rank = jnp.sum(earlier, axis=1, dtype=jnp.int32)
    slot = jnp.where(nearby > 2, nearby - 1, nearby) * CAP + rank
    pick = jnp.where(nearby == 2, len(OFFSETS) * CAP + row, slot).astype(jnp.int32)
    places = jnp.arange(len(OFFSETS) * CAP, dtype=jnp.int32)
    taken = places[:, None] == jnp.where(nearby == 2, -1, slot)[None]
    lists = jnp.sum(jnp.where(taken, row[None], 0), axis=1, dtype=jnp.int32)
    lists = jnp.pad(lists.reshape(len(OFFSETS), 1, CAP), ((0, 0), (0, 7), (0, 128 - CAP)))

    field = tracers.reshape(GROUPS, channels, tile_rows, tile_cols).transpose(0, 2, 1, 3)
    kv_all = jnp.pad(kv, ((0, 1), (0, 0), (0, 0))).transpose(1, 0, 2)
    kv_all = jnp.tile(kv_all, (1, tracer_count // GROUPS, 1))
    bf16, f32, i32 = jnp.bfloat16, jnp.float32, jnp.int32
    vmem = pl.BlockSpec(memory_space=pltpu.VMEM)
    smem = pl.BlockSpec(memory_space=pltpu.SMEM)
    count, turns = len(OFFSETS), STEPS * GROUPS
    edge_shape = (8, tile_rows // 4 * channels)
    dma = pltpu.SemaphoreType.DMA
    out = pl.pallas_call(
        functools.partial(kernel, n_lat, n_lon),
        out_shape=jax.ShapeDtypeStruct(field.shape, bf16),
        in_specs=[smem, vmem, vmem, pl.BlockSpec(memory_space=pl.ANY), vmem, vmem],
        out_specs=vmem,
        scratch_shapes=[
            pltpu.VMEM(weights.shape, bf16),
            pltpu.VMEM((count, 8, 128), i32),
            pltpu.SMEM((count, 8, 128), i32),
            *[pltpu.VMEM((count * CAP + tile_rows, channels, tile_cols), bf16)] * turns,
            pltpu.VMEM(field.shape, bf16),
            pltpu.VMEM((turns, count * CAP, channels, tile_cols), bf16),
            pltpu.VMEM((turns, SUBSTEPS, tile_rows + 2, channels, tile_cols), f32),
            pltpu.VMEM((tile_rows, channels, tile_cols), f32),
            pltpu.VMEM((turns, SUBSTEPS) + edge_shape, f32),
            pltpu.VMEM((turns, SUBSTEPS, 2) + edge_shape, f32),
            dma, dma((count,)), dma((count,)), dma,
            dma((turns, len(CUTS) - 1, count)), dma((turns, len(CUTS) - 1, count)),
            dma((turns, SUBSTEPS, 2)), dma((turns, SUBSTEPS, 2)),
            dma((turns, SUBSTEPS, 2)), dma((turns, SUBSTEPS, 2)),
        ],
        compiler_params=pltpu.CompilerParams(
            collective_id=0, has_side_effects=True, vmem_limit_bytes=44 * 1024 * 1024
        ),
    )(pick, lists, field, weights, kv_all, kh)
    return out.transpose(0, 2, 1, 3).reshape(tracers.shape)


def solution(mesh):
    return jax.shard_map(
        functools.partial(local, mesh.shape["lat"], mesh.shape["lon"]),
        mesh=mesh,
        in_specs=(
            P(None, None, "lat", "lon"),
            P("lat", None, "lon", None),
            P("lat", "lon", None),
            P("lat", "lon", None),
            P(None, "lat", "lon"),
            P("lat", "lon"),
        ),
        out_specs=P(None, None, "lat", "lon"),
        check_vma=False,
    )
```

time: 105 us -> 88.5 us (0.84)
  Pallas kernels: 98 us -> 82.7 us
  local copies, waits for them, and re-layouts: 5.11 us -> 3.89 us
    pallas_call x1, Pallas kernels: 98 us -> 82.7 us  [local(): pl.pallas_call(functools.partial(kernel, n_lat, n_lon), out_shape=jax.Sha...]
where the time goes in v2:
time: 88.5 us; the launch traced here: 88.4 us
  Pallas kernels  82.7 us (93%)
  local copies, waits for them, and re-layouts  3.89 us (4%)
  other arithmetic  1.74 us (2%)
    pallas_call x1, Pallas kernels, local(): pl.pallas_call(functools.partial(kernel, n_lat, n_lon), out_shape=jax.Sha...  82.7 us

profile of v2, /device:TPU:0, one launch (start us, length us, event | category | flops | bytes accessed | tf_op | source)
XLA Modules:
  0.0 88.4 jit_solution(258761294440475480)
XLA Ops:
  0.0 0.0 copy-start.1
  0.0 0.0 copy-start.2
  0.0 0.8 broadcast_subtract_fusion
  0.8 0.7 subtract_add_fusion
  1.4 0.1 copy.17
  1.5 0.1 add.64
  1.7 0.2 convert_reduce_fusion
  1.9 0.1 copy.18
  2.0 0.1 sub.39
  2.1 0.1 select_reduce_fusion
  2.3 0.1 reshape.72
  2.3 0.0 copy-start
  2.4 1.2 %pad_bitcast_fusion = f32[64,12,128]{2,0,1:T(8,128)S(1)} fusion(f32[11,64,128]{2,1,0:T(8,128)} %param.10), kind=kLoop, calls=%fused_computation.1 | loop fusion | bytes 753664 | tf_op jit(solution)/shard_map/transpose | solution.py:237
  3.5 0.1 tile.4
  3.6 0.5 copy.21.kv_ref
  4.1 0.0 copy-done.2
  4.1 0.5 copy.24
  4.6 0.0 copy-done.1
  4.6 0.0 copy-done
  4.6 82.7 %shard_map.64 = bf16[2,64,24,128]{3,2,1,0:T(8,128)(2,1)S(1)} custom-call(s32[128]{0:T(128)S(1)} %get-tuple-element.6.pick_ref, s32[4,8,128]{2,1,0:T(8,128)S(1)} %pad.8.list_ref, bf16[2,64,24,128]{3,2,1,0:T(8,128)(2,1)S(1)} %bitcast.15, bf16[64,2,128,128]{3,2,1,0:T(8,128)(2,1)S(1)} %copy-done, f32[64,24,128]{2,1,0:T(8,128)S(1)} %copy.21.kv_ref, ...), custom_call_target="tpu_custom_call" | custom-call | tf_op jit(solution)/shard_map/pallas_call | solution.py:245
  87.3 1.1 %copy.22 = bf16[2,24,64,128]{3,2,1,0:T(8,128)(2,1)} copy(bf16[2,24,64,128]{3,1,2,0:T(8,128)(2,1)S(1)} %bitcast.14) | data formatting | bytes 1572864 | tf_op jit(solution)/shard_map/transpose | solution.py:270
  (3 shorter events, 0.0 us)
Async XLA Ops:
  0.0 4.6 %copy-start.1 = (f32[64,128]{1,0:T(8,128)S(1)}, f32[64,128]{1,0:T(8,128)}, u32[]{:S(2)}) copy-start(f32[64,128]{1,0:T(8,128)} %kh_ref.1) | copy-start | bytes 98308
  0.0 4.1 %copy-start.2 = (bf16[4,12,64,128]{3,2,1,0:T(8,128)(2,1)S(1)}, bf16[4,12,64,128]{3,2,1,0:T(8,128)(2,1)}, u32[]{:S(2)}) copy-start(bf16[4,12,64,128]{3,2,1,0:T(8,128)(2,1)} %param.6) | copy-start | bytes 2359300
  2.3 2.3 %copy-start = (bf16[64,2,128,128]{3,2,1,0:T(8,128)(2,1)S(1)}, bf16[64,2,128,128]{3,2,1,0:T(8,128)(2,1)}, u32[]{:S(2)}) copy-start(bf16[64,2,128,128]{3,2,1,0:T(8,128)(2,1)} %weights_ref.1) | copy-start | bytes 12582916

commit v3 on v2

--- a/solution.py
+++ b/solution.py
@@ -12,7 +12,7 @@
 OFFSETS = (-2, -1, 1, 2)
 CAP = 32
 GROUPS = 2
-CUTS = (0, 8, 20, 32)
+CUTS = (0, 12, 24, 32)
 MESH = pl.DeviceIdType.MESH
 CONTRACT_LAST = (((1,), (1,)), ((), ()))
 CONTRACT_FIRST = (((0,), (0,)), ((), ()))

time: 88.5 us -> 91.6 us (1.035)
  Pallas kernels: 82.7 us -> 85.8 us
    pallas_call x1, Pallas kernels: 82.7 us -> 85.8 us  [local(): pl.pallas_call(functools.partial(kernel, n_lat, n_lon), out_shape=jax.Sha...]
where the time goes in v3:
time: 91.6 us; the launch traced here: 91.5 us
  Pallas kernels  85.8 us (94%)
  local copies, waits for them, and re-layouts  3.89 us (4%)
  other arithmetic  1.74 us (2%)
    pallas_call x1, Pallas kernels, local(): pl.pallas_call(functools.partial(kernel, n_lat, n_lon), out_shape=jax.Sha...  85.8 us

profile of v3, /device:TPU:0, one launch (start us, length us, event | category | flops | bytes accessed | tf_op | source)
XLA Modules:
  0.0 91.5 jit_solution(15453083346889208721)
XLA Ops:
  0.0 0.0 copy-start.1
  0.0 0.0 copy-start.2
  0.0 0.8 broadcast_subtract_fusion
  0.8 0.7 subtract_add_fusion
  1.4 0.1 copy.17
  1.5 0.1 add.64
  1.7 0.2 convert_reduce_fusion
  1.9 0.1 copy.18
  2.0 0.1 sub.39
  2.1 0.1 select_reduce_fusion
  2.3 0.1 reshape.72
  2.3 0.0 copy-start
  2.4 1.2 %pad_bitcast_fusion = f32[64,12,128]{2,0,1:T(8,128)S(1)} fusion(f32[11,64,128]{2,1,0:T(8,128)} %param.10), kind=kLoop, calls=%fused_computation.1 | loop fusion | bytes 753664 | tf_op jit(solution)/shard_map/transpose | solution.py:237
  3.5 0.1 tile.4
  3.6 0.5 copy.21.kv_ref
  4.1 0.0 copy-done.2
  4.1 0.5 copy.24
  4.6 0.0 copy-done.1
  4.6 0.0 copy-done
  4.6 85.8 %shard_map.64 = bf16[2,64,24,128]{3,2,1,0:T(8,128)(2,1)S(1)} custom-call(s32[128]{0:T(128)S(1)} %get-tuple-element.6.pick_ref, s32[4,8,128]{2,1,0:T(8,128)S(1)} %pad.8.list_ref, bf16[2,64,24,128]{3,2,1,0:T(8,128)(2,1)S(1)} %bitcast.15, bf16[64,2,128,128]{3,2,1,0:T(8,128)(2,1)S(1)} %copy-done, f32[64,24,128]{2,1,0:T(8,128)S(1)} %copy.21.kv_ref, ...), custom_call_target="tpu_custom_call" | custom-call | tf_op jit(solution)/shard_map/pallas_call | solution.py:245
  90.4 1.1 %copy.22 = bf16[2,24,64,128]{3,2,1,0:T(8,128)(2,1)} copy(bf16[2,24,64,128]{3,1,2,0:T(8,128)(2,1)S(1)} %bitcast.14) | data formatting | bytes 1572864 | tf_op jit(solution)/shard_map/transpose | solution.py:270
  (3 shorter events, 0.0 us)
Async XLA Ops:
  0.0 4.6 %copy-start.1 = (f32[64,128]{1,0:T(8,128)S(1)}, f32[64,128]{1,0:T(8,128)}, u32[]{:S(2)}) copy-start(f32[64,128]{1,0:T(8,128)} %kh_ref.1) | copy-start | bytes 98308
  0.0 4.1 %copy-start.2 = (bf16[4,12,64,128]{3,2,1,0:T(8,128)(2,1)S(1)}, bf16[4,12,64,128]{3,2,1,0:T(8,128)(2,1)}, u32[]{:S(2)}) copy-start(bf16[4,12,64,128]{3,2,1,0:T(8,128)(2,1)} %param.6) | copy-start | bytes 2359300
  2.3 2.3 %copy-start = (bf16[64,2,128,128]{3,2,1,0:T(8,128)(2,1)S(1)}, bf16[64,2,128,128]{3,2,1,0:T(8,128)(2,1)}, u32[]{:S(2)}) copy-start(bf16[64,2,128,128]{3,2,1,0:T(8,128)(2,1)} %weights_ref.1) | copy-start | bytes 12582916
